TPU v7x, 512 devices: a whole 4x8x8 slice. The times are simulated.
512 devices in a mesh: row: 16 (over x, z_lo), col: 32 (over z_hi, y, core).
Axes of the slice: x: 4, y: 8, z: 8 (z_hi: 2, z_lo: 4; z = z_hi * 4 + z_lo), core: 2. Of those that a mesh axis runs over, the one named last changes fastest.
Arguments:
- integrals: float32 [16, 256, 32, 256], P('row', None, 'col'), may hold values from -0.0625 to 0.0625
- amplitudes: float32 [32, 256, 16, 256], P('row', 'col'), may hold values from -6 to 6
Outputs:
- cycle: float32 [4096, 4096], P('row', 'col')
All inputs are finite; a program needn't handle non-finite values.
Results may differ from a plain program's by a relative error of at most 0.00007.
Values sent between devices are 32-bit elements; how exact they have to be, the bound alone decides.
A program may use at most 64 MiB of HBM per device.

v0:
```python
import jax
import jax.numpy as jnp
from jax import lax
from jax.sharding import PartitionSpec as P


def multiply(first, second):
    return jnp.dot(
        first, second, precision=lax.Precision.HIGHEST, preferred_element_type=jnp.float32
    )


def body(integrals, amplitudes):
    rows_count = lax.axis_size("row")
    cols_count = lax.axis_size("col")
    virtual = integrals.shape[1]
    tile_rows = integrals.shape[0] * virtual
    tile_inner = integrals.shape[2] * virtual
    integral_tile = integrals.reshape(tile_rows, tile_inner)
    occupied_here = amplitudes.shape[0]
    pair_count = amplitudes.shape[2] * amplitudes.shape[3]
    tile_cols = pair_count // cols_count
    per_row = cols_count // rows_count
    sectioned = amplitudes.reshape(occupied_here, amplitudes.shape[1], cols_count, tile_cols)
    moved = lax.all_to_all(sectioned, "col", split_axis=2, concat_axis=1, tiled=True)
    amplitude_tile = moved.reshape(occupied_here * virtual, tile_cols)
    amplitude_full = lax.all_gather(amplitude_tile, "row", axis=0, tiled=True)
    product = multiply(lax.all_gather(integral_tile, "col", axis=1, tiled=True), amplitude_full)
    column_part = tile_cols // rows_count
    shaped = product.reshape(per_row, tile_cols, rows_count, column_part)
    routed = lax.all_to_all(
        lax.all_to_all(shaped, "row", split_axis=2, concat_axis=0, tiled=True),
        "col",
        split_axis=0,
        concat_axis=2,
        tiled=True,
    )
    returned = lax.all_to_all(routed, "row", split_axis=2, concat_axis=0, tiled=True)
    mirror = jnp.transpose(returned, (2, 0, 3, 1)).reshape(tile_rows, tile_cols)
    return product + mirror


def solution(mesh):
    return jax.shard_map(
        body,
        mesh=mesh,
        in_specs=(P("row", None, "col", None), P("row", "col", None, None)),
        out_specs=P("row", "col"),
        check_vma=False,
    )
```

profile of v0, /device:TPU:57, one launch (start us, length us, event | category | flops | bytes accessed | tf_op | source)
XLA Modules:
  0.0 377.5 jit_solution(9401183175384466128)
XLA Ops:
  6.5 0.0 all-gather.4.cloned.1.call-start
  6.5 1.0 reshape.17
  7.5 0.2 copy.10
  7.7 28.6 %all_to_all.69 = f32[2,8,32,128]{3,1,0,2:T(8,128)S(1)} all-to-all(f32[2,8,32,128]{3,1,0,2:T(8,128)S(1)} %copy.10), channel_id=1, replica_groups=mesh['row'=16,'col'=32] {'col'}, dimensions={2} | all-to-all | bytes 524288 | tf_op jit(solution)/shard_map/all_to_all | solution.py:25
  36.3 0.7 copy.11
  37.0 0.0 all-gather.4.cloned.1.call-update
  37.0 0.0 all-gather.6.cloned.1.call-start
  37.1 0.7 all-gather.6.cloned.1.call-update
  37.8 101.6 %all-gather.4.cloned.1.call-done = f32[8192,128]{1,0:T(8,128)} async-done(((f32[512,128]{1,0:T(8,128)}), f32[8192,128]{1,0:T(8,128)}) %all-gather.4.cloned.1.call-update) | async-done | bytes 4194320 | tf_op jit(solution)/shard_map/all_gather | solution.py:27
  139.4 174.7 %all-gather.6.cloned.1.call-done = f32[1,256,1,8192]{3,2,1,0:T(1,128)} async-done(((f32[1,256,1,256]{3,2,1,0:T(1,128)}), f32[1,256,1,8192]{3,2,1,0:T(1,128)}) %all-gather.6.cloned.1.call-update) | async-done | bytes 8388624 | tf_op jit(solution)/shard_map/all_gather | solution.py:28
  314.1 14.8 %fusion = f32[256,128]{1,0:T(8,128)S(1)} fusion(f32[8192,128]{1,0:T(8,128)} %all-gather.4.cloned.1.call-done, f32[1,256,1,8192]{3,2,1,0:T(1,128)} %all-gather.6.cloned.1.call-done), kind=kOutput, calls=%fused_computation | convolution fusion | flops 3221225472 | bytes 12713984 | tf_op jit(solution)/shard_map/dot_general | solution.py:8
  328.9 0.1 copy.12
  329.0 0.1 reshape.19
  329.1 11.9 %all_to_all.70 = f32[2,128,16,8]{1,0,3,2:T(2,128)S(1)} all-to-all(f32[2,128,16,8]{1,0,3,2:T(2,128)S(1)} %reshape.19), channel_id=1, replica_groups=mesh['row'=16,'col'=32] {'row'}, dimensions={2} | all-to-all | bytes 262144 | tf_op jit(solution)/shard_map/all_to_all | solution.py:32
  340.9 19.1 %all_to_all.71 = f32[32,128,1,8]{1,3,2,0:T(8,128)S(1)} all-to-all(f32[32,128,1,8]{1,3,2,0:T(8,128)S(1)} %bitcast.35), channel_id=1, replica_groups=mesh['row'=16,'col'=32] {'col'}, dimensions={0} | all-to-all | bytes 262144 | tf_op jit(solution)/shard_map/all_to_all | solution.py:31
  360.1 9.9 %all_to_all.72 = f32[1,128,32,8]{1,3,0,2:T(8,128)S(1)} all-to-all(f32[1,128,32,8]{1,3,0,2:T(8,128)S(1)} %bitcast.36), channel_id=1, replica_groups=mesh['row'=16,'col'=32] {'row'}, dimensions={2} | all-to-all | bytes 262144 | tf_op jit(solution)/shard_map/all_to_all | solution.py:38
  370.0 0.7 bitcast_add_fusion
  (2 shorter events, 0.0 us)
Async XLA Ops:
  6.5 132.9 %all-gather.4.cloned.1.call-start = ((), (), s32[]{:S(2)}) async-start(), calls=%async_computation.4 | async-start | bytes 4456448 | tf_op jit(solution)/shard_map/all_gather | solution.py:27
  37.0 277.1 %all-gather.6.cloned.1.call-start = ((), (), s32[]{:S(2)}) async-start(), calls=%async_computation.5 | async-start | bytes 8650752 | tf_op jit(solution)/shard_map/all_gather | solution.py:28
Sparse Core Ops, SparseCore 0:
  37.2 102.2 all-gather.3
  142.5 171.5 all-gather.5
where the time goes:
time: 381 us; the launch traced here: 377 us
  waiting for transfers between devices  277 us (73%)
  blocking collectives  69.5 us (18%)
  matrix products  14.8 us (4%)
  between operations  13.4 us (4%)
    all_gather x1, waiting for transfers between devices, body(): lax.all_gather(integral_tile, 'col', axis=1, tiled=True)  175 us
    all_gather x1, waiting for transfers between devices, body(): amplitude_full = lax.all_gather(amplitude_tile, 'row', axis=0, tiled=True)  102 us
    all_to_all x1, blocking collectives, body(): lax.all_to_all(sectioned, 'col', split_axis=2, concat_axis=1, tiled=True)  28.6 us
    all_to_all x1, blocking collectives, body(): lax.all_to_all(lax.all_to_all(shaped, 'row', split_axis=2, concat_axis=0,...  19.1 us
    dot_general x1, matrix products, multiply(): jnp.dot(first, second, precision=lax.Precision.HIGHEST, preferred_element...  14.8 us
    all_to_all x1, blocking collectives, body(): lax.all_to_all(shaped, 'row', split_axis=2, concat_axis=0, tiled=True)  11.9 us
    all_to_all x1, blocking collectives, body(): lax.all_to_all(routed, 'row', split_axis=2, concat_axis=0, tiled=True)  9.86 us
  transfers between devices with their start and end apart: 2, of which 2 were waited for; matrix products, arithmetic and copies ran while one was open for 0% of the time, Pallas kernels for 0%

commit v1 on v0

v1 whole, which is shorter than its diff:
```python
import jax
import jax.numpy as jnp
from jax import lax
from jax.experimental import pallas as pl
from jax.experimental.pallas import tpu as pltpu
from jax.sharding import PartitionSpec as P

MESH = pl.DeviceIdType.MESH
RING = 8
F32, BF16 = jnp.float32, jnp.bfloat16


def device(x, z, y, core):
    return (x * 4 + z % 4, (z // 4) * 16 + y * 2 + core)


def split(value):
    high = value.astype(BF16)
    return high, (value - high.astype(F32)).astype(BF16)


def kernel(
    left_ref, right_ref, out_ref,
    pieces, left_all, right_all, left_hi, left_lo, right_hi, right_lo,
    partial, arrived, summed, own, mirror,
    spread_send, spread_recv, move_send, move_recv,
    ysend, yrecv, zsend, zrecv, share_send, share_recv,
    part_send, part_recv, own_send, own_recv, mirror_send, mirror_recv,
):
    row, col = lax.axis_index("row"), lax.axis_index("col")
    x, zl, zh, y, core = row // 4, row % 4, col // 16, (col // 2) % 8, col % 2
    z = zh * 4 + zl
    x1, x0, zl1, zl0 = x // 2, x % 2, zl // 2, zl % 2
    y2, y1, y0 = y // 4, (y // 2) % 2, y % 2

    spread_x, spread_z = x1 * 2 + zl0, zh * 4 + zl1 * 2 + x0
    spread_home = x0 == zl0
    move_to = (zh * 2 + y0, x0 * 4 + zl, y2 * 4 + y1 * 2 + x1)
    move_from = (y0 * 2 + zh, x1 * 4 + zl, y2 * 4 + y1 * 2 + x0)
    move_home = (x1 == x0) & (x0 == zh) & (zh == y0)
    own_to = (x1 * 2 + zh, x0 * 4 + zl, y)
    own_home = x0 == zh
    mirror_to = (2 * x0 + y2, x1 * 4 + y % 4, 4 * zh + zl)
    mirror_from = (2 * zh + x1, y2 * 4 + y % 4, 4 * x0 + zl)
    mirror_home = (mirror_to[0] == x) & (mirror_to[1] == z) & (mirror_to[2] == y)

    yr, yl, zr, zlft = (y + 1) % RING, (y + 7) % RING, (z + 1) % RING, (z + 7) % RING

    barrier = pltpu.get_barrier_semaphore()

    def greet(target):
        pl.semaphore_signal(barrier, inc=1, device_id=target, device_id_type=MESH)

    greet(device(x, z, yr, core))
    greet(device(x, z, yl, core))
    greet(device(x, zr, y, core))
    greet(device(x, zlft, y, core))
    greet(device(x, z, y, 1 - core))
    for dx in range(1, 4):
        greet(device((x + dx) % 4, z, y, core))
    for dy in range(8):
        for de in range(2):
            target = device(spread_x, spread_z, (y + dy) % 8, (core + de) % 2)
            if dy == 0 and de == 0:
                @pl.when(jnp.logical_not(spread_home))
                def _():
                    greet(target)
            else:
                greet(target)

    @pl.when(jnp.logical_not(move_home))
    def _():
        greet(device(*move_from, core))

    for k in range(2):
        for high in range(2):
            for e in range(2):
                block = right_ref[k, :, 8 * high : 8 * high + 8, 128 * e : 128 * e + 128]
                block = jnp.swapaxes(block, 0, 1)
                for j in range(8):
                    pieces[j, e, k, :, 128 * high : 128 * high + 128] = block[j]

    away = jnp.logical_not(move_home).astype(jnp.int32) + jnp.logical_not(spread_home).astype(jnp.int32)
    pl.semaphore_wait(barrier, 23 + away)

    sends = []

    def copy(src, dst, send_sem, recv_sem, target):
        return pltpu.make_async_remote_copy(
            src_ref=src, dst_ref=dst, send_sem=send_sem, recv_sem=recv_sem,
            device_id=target, device_id_type=MESH,
        )

    def start(*args):
        made = copy(*args)
        made.start()
        sends.append(made)

    def arrive(ref, sem):
        pltpu.make_async_copy(ref, ref, sem).wait()

    for dy in (0, 1, 7, 2, 6, 3, 5, 4):
        for de in range(2):
            ty, te = (y + dy) % 8, (core + de) % 2
            src = pieces.at[ty, te]
            place = pl.ds(pl.multiple_of(16 * y + 8 * core, 8), 8)
            dst = right_all.at[spread_z, :, place, :]
            made = copy(src, dst, spread_send.at[dy * 2 + de], spread_recv, device(spread_x, spread_z, ty, te))
            if dy == 0 and de == 0:
                @pl.when(spread_home)
                def _():
                    pltpu.make_async_copy(src, dst, spread_recv).start()

                @pl.when(jnp.logical_not(spread_home))
                def _():
                    made.start()
            else:
                made.start()
                sends.append(made)
            if dy == 0 and de == 0:
                first = made

    moves = []
    for h in range(2):
        src = left_ref.at[pl.ds(128 * h, 128)]
        dst = left_all.at[move_to[2], core, h]
        made = copy(src, dst, move_send.at[h], move_recv.at[h], device(*move_to, core))
        moves.append(made)

        @pl.when(move_home)
        def _():
            pltpu.make_async_copy(src, dst, move_recv.at[h]).start()

        @pl.when(jnp.logical_not(move_home))
        def _():
            made.start()

    def send_y(slot, h, way, step):
        ref = left_all.at[slot, core, h]
        start(ref, ref, ysend.at[way, step, h], yrecv.at[way, step, h], device(x, z, yr if way == 0 else yl, core))

    def send_z(slot, h, way, step):
        ref = right_all.at[slot, h]
        start(ref, ref, zsend.at[way, step, h], zrecv.at[way, step, h], device(x, zr if way == 0 else zlft, y, core))

    def share(slot, h, number):
        ref = left_all.at[slot, core, h]
        start(ref, ref, share_send.at[number], share_recv.at[number], device(x, z, y, 1 - core))

    def split_left(slot, e, h):
        left_hi[slot, e, h], left_lo[slot, e, h] = split(left_all[slot, e, h])

    def split_right(slot, k):
        part = slot // 4
        kind = (slot % 2) * 2 + (slot // 2) % 2
        half = pl.ds(pl.multiple_of(128 * part, 128), 128)
        right_hi[kind, k, half, :], right_lo[kind, k, half, :] = split(right_all[slot, k])

    arrive(right_all.at[z], spread_recv)
    for i in range(2):
        send_z(z, i, 0, 0)
        send_z(z, 1 - i, 1, 0)
    for h in range(2):
        arrive(left_all.at[y, core, h], move_recv.at[h])
        send_y(y, h, 0, 0)
        send_y(y, h, 1, 0)
        share(y, h, h)
    for k in range(2):
        split_right(z, k)
    for h in range(2):
        split_left(y, core, h)
    shared = [(y, 0), (y, 1)]
    for step in range(4):
        for i in range(2):
            for way in range(2):
                h = i if way == 0 else 1 - i
                if step == 3 and i == 1:
                    continue
                last = step == 3 or (step == 2 and i == 1)
                slot = (z - 1 - step + 8) % 8 if way == 0 else (z + 1 + step) % 8
                arrive(right_all.at[slot, h], zrecv.at[way, step, h])
                if not last:
                    send_z(slot, h, way, step + 1)
                slot_y = (y - 1 - step + 8) % 8 if way == 0 else (y + 1 + step) % 8
                arrive(left_all.at[slot_y, core, h], yrecv.at[way, step, h])
                if not last:
                    send_y(slot_y, h, way, step + 1)
                share(slot_y, h, len(shared))
                shared.append((slot_y, h))
                split_right(slot, h)
                split_left(slot_y, core, h)
    for number, (slot_y, h) in enumerate(shared):
        arrive(left_all.at[slot_y, 1 - core, h], share_recv.at[number])
        split_left(slot_y, 1 - core, h)

    parts = []
    for h in range(2):
        for f in range(2):
            total = jnp.zeros((128, 256), F32)
            for kind in range(4):
                slot_y = (kind // 2) * 4 + (kind % 2) * 2 + f
                for e in range(2):
                    lh, ll = left_hi[slot_y, e, h], left_lo[slot_y, e, h]
                    rh, rl = right_hi[kind, e], right_lo[kind, e]
                    total += jnp.dot(lh, rh, preferred_element_type=F32)
                    total += jnp.dot(lh, rl, preferred_element_type=F32)
                    total += jnp.dot(ll, rh, preferred_element_type=F32)
            partial[2 * f, h] = total[:, :128]
            partial[2 * f + 1, h] = total[:, 128:]
        for dx in range(1, 4):
            tx = (x + dx) % 4
            start(partial.at[tx, h], arrived.at[dx - 1, h], part_send.at[dx - 1, h], part_recv.at[dx - 1, h],
                  device(tx, z, y, core))

    owns = []
    for h in range(2):
        for d in range(3):
            arrive(arrived.at[d, h], part_recv.at[d, h])
        summed[h] = partial[x, h] + arrived[0, h] + arrived[1, h] + arrived[2, h]
        made_own = copy(summed.at[h], own.at[h], own_send.at[h], own_recv.at[h], device(*own_to, core))
        made_mirror = copy(summed.at[h], mirror.at[core], mirror_send.at[h], mirror_recv.at[core],
                           device(*mirror_to, h))
        at_home = mirror_home & (core == h)
        owns.append((made_own, made_mirror, at_home))

        @pl.when(own_home)
        def _():
            pltpu.make_async_copy(summed.at[h], own.at[h], own_recv.at[h]).start()

        @pl.when(jnp.logical_not(own_home))
        def _():
            made_own.start()

        @pl.when(at_home)
        def _():
            pltpu.make_async_copy(summed.at[h], mirror.at[core], mirror_recv.at[core]).start()

        @pl.when(jnp.logical_not(at_home))
        def _():
            made_mirror.start()

    for h in range(2):
        arrive(own.at[h], own_recv.at[h])
    for e in range(2):
        arrive(mirror.at[e], mirror_recv.at[e])
        out_ref[128 * e : 128 * e + 128, :] = own[e] + jnp.transpose(mirror[e])

    for made in sends:
        made.wait_send()

    @pl.when(jnp.logical_not(spread_home))
    def _():
        first.wait_send()

    for h in range(2):
        @pl.when(jnp.logical_not(move_home))
        def _():
            moves[h].wait_send()

        made_own, made_mirror, at_home = owns[h]

        @pl.when(jnp.logical_not(own_home))
        def _():
            made_own.wait_send()

        @pl.when(jnp.logical_not(at_home))
        def _():
            made_mirror.wait_send()


def body(integrals, amplitudes):
    dma = pltpu.SemaphoreType.DMA
    return pl.pallas_call(
        kernel,
        out_shape=jax.ShapeDtypeStruct((256, 128), F32),
        in_specs=[pl.BlockSpec(memory_space=pl.ANY), pl.BlockSpec(memory_space=pltpu.VMEM)],
        out_specs=pl.BlockSpec(memory_space=pltpu.VMEM),
        scratch_shapes=[
            pltpu.VMEM((8, 2, 2, 8, 256), F32),
            pltpu.VMEM((8, 2, 2, 128, 256), F32),
            pltpu.VMEM((8, 2, 128, 256), F32),
            pltpu.VMEM((8, 2, 2, 128, 256), BF16),
            pltpu.VMEM((8, 2, 2, 128, 256), BF16),
            pltpu.VMEM((4, 2, 256, 256), BF16),
            pltpu.VMEM((4, 2, 256, 256), BF16),
            pltpu.VMEM((4, 2, 128, 128), F32),
            pltpu.VMEM((3, 2, 128, 128), F32),
            pltpu.VMEM((2, 128, 128), F32),
            pltpu.VMEM((2, 128, 128), F32),
            pltpu.VMEM((2, 128, 128), F32),
            dma((16,)), dma,
            dma((2,)), dma((2,)),
            dma((2, 4, 2)), dma((2, 4, 2)),
            dma((2, 4, 2)), dma((2, 4, 2)),
            dma((16,)), dma((16,)),
            dma((3, 2)), dma((3, 2)),
            dma((2,)), dma((2,)),
            dma((2,)), dma((2,)),
        ],
        compiler_params=pltpu.CompilerParams(
            collective_id=0, has_side_effects=True, vmem_limit_bytes=40 << 20
        ),
        cost_estimate=pl.CostEstimate(flops=3 * 2**29, bytes_accessed=1 << 20, transcendentals=0),
        name="cycle",
    )(integrals.reshape(256, 256), amplitudes)


def solution(mesh):
    return jax.shard_map(
        body,
        mesh=mesh,
        in_specs=(P("row", None, "col", None), P("row", "col", None, None)),
        out_specs=P("row", "col"),
        check_vma=False,
    )
```

time: 381 us -> 97.9 us (0.26)
  waiting for transfers between devices: 277 us -> 0 us
  Pallas kernels: 0 us -> 96.1 us
  blocking collectives: 69.5 us -> 0 us
  matrix products: 14.8 us -> 0 us
  between operations: 13.4 us -> 0.01 us
    all_gather x2 -> x0, waiting for transfers between devices: 276 us -> none  [the longest x1 175 us: body(): lax.all_gather(integral_tile, 'col', axis=1, tiled=True)]
    pallas_call x0 -> x1, Pallas kernels: none -> 96.1 us  [body(): pl.pallas_call(kernel, out_shape=jax.ShapeDtypeStruct((256, 128), F32), i...]
    all_to_all x4 -> x0, blocking collectives: 69.5 us -> none  [the longest x1 28.6 us: body(): lax.all_to_all(sectioned, 'col', split_axis=2, concat_axis=1, tiled=True)]
    dot_general x1 -> x0, matrix products: 14.8 us -> none  [multiply(): jnp.dot(first, second, precision=lax.Precision.HIGHEST, preferred_element...]
  transfers between devices with their start and end apart: 2 -> 0, of which waited for: 2 -> 0; matrix products, arithmetic and copies ran while one was open for 0% -> 0% of each run, Pallas kernels for 0% -> 0%
where the time goes in v1:
time: 97.9 us; the launch traced here: 97.8 us
  Pallas kernels  96.1 us (98%)
  local copies, waits for them, and re-layouts  1.68 us (2%)
    pallas_call x1, Pallas kernels, body(): pl.pallas_call(kernel, out_shape=jax.ShapeDtypeStruct((256, 128), F32), i...  96.1 us

profile of v1, /device:TPU:57, one launch (start us, length us, event | category | flops | bytes accessed | tf_op | source)
XLA Modules:
  0.0 97.8 jit_solution(2544872238741852885)
XLA Ops:
  0.0 0.0 copy-start
  0.0 1.0 %copy.5 = f32[1,256,1,256]{3,1,2,0:T(8,128)S(1)} copy(f32[1,256,1,256]{3,2,1,0:T(1,128)} %param.2) | data formatting | bytes 524288
  1.0 0.0 copy-done
  1.0 96.1 %cycle.1 = f32[256,128]{1,0:T(8,128)S(1)} custom-call(f32[256,256]{1,0:T(8,128)S(1)} %bitcast.3, f32[2,8,16,256]{3,2,1,0:T(8,128)S(1)} %copy-done), custom_call_target="tpu_custom_call" | custom-call | flops 1610612736 | bytes 1048576 | tf_op jit(solution)/shard_map/cycle/pallas_call | solution.py:273
  97.1 0.7 copy.7
Async XLA Ops:
  0.0 1.0 %copy-start = (f32[2,8,16,256]{3,2,1,0:T(8,128)S(1)}, f32[2,8,16,256]{3,2,1,0:T(8,128)}, u32[]{:S(2)}) copy-start(f32[2,8,16,256]{3,2,1,0:T(8,128)} %right_ref.1) | copy-start | bytes 786436

commit v2 on v0

v2 whole, which is shorter than its diff:
```python
import jax
import jax.numpy as jnp
from jax import lax
from jax.experimental import pallas as pl
from jax.experimental.pallas import tpu as pltpu
from jax.sharding import PartitionSpec as P

MESH = pl.DeviceIdType.MESH
RING = 8
F32, BF16 = jnp.float32, jnp.bfloat16


def device(x, z, y, core):
    return (x * 4 + z % 4, (z // 4) * 16 + y * 2 + core)


def split(value):
    high = value.astype(BF16)
    return high, (value - high.astype(F32)).astype(BF16)


def dot(first, second):
    return jnp.dot(first, second, preferred_element_type=F32)


def kernel(
    left_ref, right_ref, out_ref,
    packed, stage, far, left_all, pieces, rows_here, right_all, left_hi, left_lo, right_hi, right_lo,
    partial, arrived, summed, own, mirror,
    pack_send, pack_recv, far_send, far_recv, spread_send, spread_recv, third_send, third_recv,
    ysend, yrecv, zsend, zrecv, share_send, share_recv,
    part_send, part_recv, own_send, own_recv, mirror_send, mirror_recv,
):
    row, col = lax.axis_index("row"), lax.axis_index("col")
    x, zl, zh, y, core = row // 4, row % 4, col // 16, (col // 2) % 8, col % 2
    z = zh * 4 + zl
    x1, x0 = x // 2, x % 2

    barrier = pltpu.get_barrier_semaphore()

    def greet(*target):
        pl.semaphore_signal(barrier, inc=1, device_id=device(*target), device_id_type=MESH)

    for dx in range(1, 4):
        greet((x + dx) % 4, z, y, core)
    for dz in (1, 7, 4):
        greet(x, (z + dz) % 8, y, core)
    for dy in range(8):
        for de in range(2):
            if dy or de:
                greet(x, z, (y + dy) % 8, (core + de) % 2)

    for half in range(2):
        for k in range(2):
            for e in range(2):
                block = right_ref[k, :, 8 * half : 8 * half + 8, 128 * e : 128 * e + 128]
                block = jnp.swapaxes(block, 0, 1)
                for j in range(8):
                    pieces[half, j, e, k] = block[j]

    c = lax.broadcasted_iota(jnp.int32, (256, 512), 0)
    t = lax.broadcasted_iota(jnp.int32, (256, 512), 1)
    place = (c // 32) % 4 * 128 + c // 128 * 32 + c % 32
    pick = [(t == place + shift).astype(F32).astype(BF16) for shift in (0, 64)]
    quarters = jnp.zeros((128, 512), F32)
    for i in range(2):
        begin = pl.multiple_of(128 * (zh if i == 0 else 1 - zh), 128)
        high, low = split(left_ref[pl.ds(begin, 128), :])
        quarters += dot(high, pick[i]) + dot(low, pick[i])
    for q in range(4):
        packed[q] = quarters[:, 128 * q : 128 * q + 128]

    pl.semaphore_wait(barrier, 21)

    sends = []
    maybe = []

    def copy(src, dst, send_sem, recv_sem, target):
        return pltpu.make_async_remote_copy(
            src_ref=src, dst_ref=dst, send_sem=send_sem, recv_sem=recv_sem,
            device_id=device(*target), device_id_type=MESH,
        )

    def start(*args):
        made = copy(*args)
        made.start()
        sends.append(made)

    def start_or_keep(home, src, dst, send_sem, recv_sem, target):
        made = copy(src, dst, send_sem, recv_sem, target)

        @pl.when(home)
        def _():
            pltpu.make_async_copy(src, dst, recv_sem).start()

        @pl.when(jnp.logical_not(home))
        def _():
            made.start()

        maybe.append((home, made))

    def arrive(ref, sem):
        pltpu.make_async_copy(ref, ref, sem).wait()

    def spread(half):
        mine = pl.ds(pl.multiple_of(16 * y + 8 * core, 8), 8)
        dst = rows_here.at[half, :, mine, :]
        for dy in (1, 7, 2, 6, 3, 5, 4, 0):
            for de in range(2):
                ty, te = (y + dy) % 8, (core + de) % 2
                src = pieces.at[half, ty, te]
                if dy or de:
                    start(src, dst, spread_send.at[half, dy * 2 + de], spread_recv.at[half], (x, z, ty, te))
                else:
                    pltpu.make_async_copy(src, dst, spread_recv.at[half]).start()

    def spread_x(half):
        for dx in range(4):
            tx = (x + dx) % 4
            src = rows_here.at[half, :, pl.ds(pl.multiple_of(32 * tx, 32), 32), :]
            dst = right_all.at[z, half, x]
            if dx:
                start(src, dst, third_send.at[half, dx], third_recv.at[half], (tx, z, y, core))
            else:
                pltpu.make_async_copy(src, dst, third_recv.at[half]).start()

    spread(0)
    goes = (x1 != zh).astype(jnp.int32)
    for dx in range(4):
        tx = (x + dx) % 4
        dst = stage.at[goes, x0]
        if dx:
            start(packed.at[tx], dst, pack_send.at[dx], pack_recv.at[goes], (tx, z, y, core))
        else:
            pltpu.make_async_copy(packed.at[tx], dst, pack_recv.at[goes]).start()
    spread(1)
    arrive(stage.at[1], pack_recv.at[1])
    start(stage.at[1], far, far_send, far_recv, (x, (z + 4) % 8, y, core))
    arrive(rows_here.at[0], spread_recv.at[0])
    spread_x(0)
    arrive(rows_here.at[1], spread_recv.at[1])
    spread_x(1)

    yr, yl, zr, zlft = (y + 1) % RING, (y + 7) % RING, (z + 1) % RING, (z + 7) % RING

    def send_y(slot, h, way, step):
        ref = left_all.at[slot, core, h]
        start(ref, ref, ysend.at[way, step, h], yrecv.at[way, step, h], (x, z, yr if way == 0 else yl, core))

    def send_z(slot, h, way, step):
        ref = right_all.at[slot, h]
        start(ref, ref, zsend.at[way, step, h], zrecv.at[way, step, h], (x, zr if way == 0 else zlft, y, core))

    def share(slot, h, number):
        ref = left_all.at[slot, core, h]
        start(ref, ref, share_send.at[number], share_recv.at[number], (x, z, y, 1 - core))

    def split_left(slot, e, h):
        lanes = pl.ds(pl.multiple_of(128 * e, 128), 128)
        left_hi[slot, h, :, lanes], left_lo[slot, h, :, lanes] = split(left_all[slot, e, h])

    def split_right(slot, half):
        high, low = split(right_all[slot, half])
        for s3 in range(2):
            for s2 in range(2):
                for k in range(2):
                    begin = pl.multiple_of(128 * k + 64 * s3 + 32 * (slot // 4), 32)
                    at = (s2 * 4 + slot % 4, pl.ds(begin, 32), slice(128 * half, 128 * half + 128))
                    right_hi[at] = high[2 * s3 + s2, k]
                    right_lo[at] = low[2 * s3 + s2, k]

    def ring_z_begin(h):
        arrive(right_all.at[z, h], third_recv.at[h])
        send_z(z, h, h, 0)
        send_z(z, h, 1 - h, 0)

    ring_z_begin(0)
    arrive(stage.at[0], pack_recv.at[0])
    arrive(far, far_recv)
    low_lane = lax.broadcasted_iota(jnp.int32, (128, 128), 1) < 64
    for f in range(2):
        near_part, far_part = stage[0, f], far[f]
        even = jnp.where(zh == 0, near_part, far_part)
        odd = jnp.where(zh == 0, far_part, near_part)
        left_all[y, core, f, 0:128] = jnp.where(low_lane, even, odd)
        left_all[y, core, f, 128:256] = pltpu.roll(jnp.where(low_lane, odd, even), 64, 1)
        send_y(y, f, f, 0)
        send_y(y, f, 1 - f, 0)
        share(y, f, f)
    ring_z_begin(1)
    shared = [(y, 0), (y, 1)]
    for h in range(2):
        split_right(z, h)
        split_left(y, core, h)
    for step in range(4):
        for i in range(2):
            for way in range(2):
                h = i if way == 0 else 1 - i
                if step == 3 and i == 1:
                    continue
                last = step == 3 or (step == 2 and i == 1)
                slot = (z - 1 - step + 8) % 8 if way == 0 else (z + 1 + step) % 8
                arrive(right_all.at[slot, h], zrecv.at[way, step, h])
                if not last:
                    send_z(slot, h, way, step + 1)
                slot_y = (y - 1 - step + 8) % 8 if way == 0 else (y + 1 + step) % 8
                arrive(left_all.at[slot_y, core, h], yrecv.at[way, step, h])
                if not last:
                    send_y(slot_y, h, way, step + 1)
                share(slot_y, h, len(shared))
                shared.append((slot_y, h))
                split_right(slot, h)
                split_left(slot_y, core, h)
    for number, (slot_y, h) in enumerate(shared):
        arrive(left_all.at[slot_y, 1 - core, h], share_recv.at[number])
        split_left(slot_y, 1 - core, h)

    for f in range(2):
        total = jnp.zeros((256, 256), F32)
        for unit in range(8):
            lh, ll, rh, rl = left_hi[unit, f], left_lo[unit, f], right_hi[unit], right_lo[unit]
            total += dot(lh, rh) + dot(lh, rl) + dot(ll, rh)
        for half in range(2):
            partial[f, half] = total[:, 128 * half : 128 * half + 128]
        for dx in range(1, 4):
            tx = (x + dx) % 4
            src = partial.at[f, :, pl.ds(pl.multiple_of(64 * tx, 64), 64), :]
            start(src, arrived.at[dx - 1, f], part_send.at[dx - 1, f], part_recv.at[dx - 1, f], (tx, z, y, core))

    for f in range(2):
        for d in range(3):
            arrive(arrived.at[d, f], part_recv.at[d, f])
        kept = partial[f, :, pl.ds(pl.multiple_of(64 * x, 64), 64), :]
        summed[f] = kept + arrived[0, f] + arrived[1, f] + arrived[2, f]
        for half in range(2):
            src = summed.at[f, half]
            to = (2 * half + y // 4, zh * 4 + y % 4, 4 * f + zl, x // 2)
            dst = mirror.at[core, pl.ds(pl.multiple_of(64 * x0, 64), 64)]
            home = (to[0] == x) & (to[1] == z) & (to[2] == y) & (to[3] == core)
            start_or_keep(home, src, dst, mirror_send.at[f, half], mirror_recv, to)
            to = (2 * zh + f, half * 4 + zl, y, core)
            dst = own.at[pl.ds(pl.multiple_of(64 * x, 64), 64)]
            home = (to[0] == x) & (to[1] == z)
            start_or_keep(home, src, dst, own_send.at[f, half], own_recv, to)

    arrive(own, own_recv)
    arrive(mirror, mirror_recv)
    for e in range(2):
        out_ref[128 * e : 128 * e + 128, :] = own[128 * e : 128 * e + 128] + jnp.transpose(mirror[e])

    for made in sends:
        made.wait_send()
    for home, made in maybe:
        pl.when(jnp.logical_not(home))(made.wait_send)


def body(integrals, amplitudes):
    dma = pltpu.SemaphoreType.DMA
    return pl.pallas_call(
        kernel,
        out_shape=jax.ShapeDtypeStruct((256, 128), F32),
        in_specs=[pl.BlockSpec(memory_space=pltpu.VMEM), pl.BlockSpec(memory_space=pltpu.VMEM)],
        out_specs=pl.BlockSpec(memory_space=pltpu.VMEM),
        scratch_shapes=[
            pltpu.VMEM((4, 128, 128), F32),
            pltpu.VMEM((2, 2, 128, 128), F32),
            pltpu.VMEM((2, 128, 128), F32),
            pltpu.VMEM((8, 2, 2, 256, 128), F32),
            pltpu.VMEM((2, 8, 2, 2, 8, 128), F32),
            pltpu.VMEM((2, 2, 128, 128), F32),
            pltpu.VMEM((8, 2, 4, 2, 32, 128), F32),
            pltpu.VMEM((8, 2, 256, 256), BF16),
            pltpu.VMEM((8, 2, 256, 256), BF16),
            pltpu.VMEM((8, 256, 256), BF16),
            pltpu.VMEM((8, 256, 256), BF16),
            pltpu.VMEM((2, 2, 256, 128), F32),
            pltpu.VMEM((3, 2, 2, 64, 128), F32),
            pltpu.VMEM((2, 2, 64, 128), F32),
            pltpu.VMEM((256, 128), F32),
            pltpu.VMEM((2, 128, 128), F32),
            dma((4,)), dma((2,)),
            dma, dma,
            dma((2, 16)), dma((2,)),
            dma((2, 4)), dma((2,)),
            dma((2, 4, 2)), dma((2, 4, 2)),
            dma((2, 4, 2)), dma((2, 4, 2)),
            dma((16,)), dma((16,)),
            dma((3, 2)), dma((3, 2)),
            dma((2, 2)), dma,
            dma((2, 2)), dma,
        ],
        compiler_params=pltpu.CompilerParams(
            collective_id=0, has_side_effects=True, vmem_limit_bytes=40 << 20
        ),
        cost_estimate=pl.CostEstimate(flops=3 * 2**29, bytes_accessed=1 << 20, transcendentals=0),
        name="cycle",
    )(integrals.reshape(256, 256), amplitudes)


def solution(mesh):
    return jax.shard_map(
        body,
        mesh=mesh,
        in_specs=(P("row", None, "col", None), P("row", "col", None, None)),
        out_specs=P("row", "col"),
        check_vma=False,
    )
```

time: 381 us -> 75.7 us (0.20)
  waiting for transfers between devices: 277 us -> 0 us
  Pallas kernels: 0 us -> 73.6 us
  blocking collectives: 69.5 us -> 0 us
  matrix products: 14.8 us -> 0 us
  between operations: 13.4 us -> 0.01 us
    all_gather x2 -> x0, waiting for transfers between devices: 276 us -> none  [the longest x1 175 us: body(): lax.all_gather(integral_tile, 'col', axis=1, tiled=True)]
    pallas_call x0 -> x1, Pallas kernels: none -> 73.6 us  [body(): pl.pallas_call(kernel, out_shape=jax.ShapeDtypeStruct((256, 128), F32), i...]
    all_to_all x4 -> x0, blocking collectives: 69.5 us -> none  [the longest x1 28.6 us: body(): lax.all_to_all(sectioned, 'col', split_axis=2, concat_axis=1, tiled=True)]
    dot_general x1 -> x0, matrix products: 14.8 us -> none  [multiply(): jnp.dot(first, second, precision=lax.Precision.HIGHEST, preferred_element...]
  transfers between devices with their start and end apart: 2 -> 0, of which waited for: 2 -> 0; matrix products, arithmetic and copies ran while one was open for 0% -> 0% of each run, Pallas kernels for 0% -> 0%
where the time goes in v2:
time: 75.7 us; the launch traced here: 75.3 us
  Pallas kernels  73.6 us (97%)
  local copies, waits for them, and re-layouts  1.68 us (2%)
    pallas_call x1, Pallas kernels, body(): pl.pallas_call(kernel, out_shape=jax.ShapeDtypeStruct((256, 128), F32), i...  73.6 us
    unnamed x4, local copies, waits for them, and re-layouts  1.68 us

profile of v2, /device:TPU:57, one launch (start us, length us, event | category | flops | bytes accessed | tf_op | source)
XLA Modules:
  0.0 75.3 jit_solution(9187649880582804539)
XLA Ops:
  0.0 0.0 copy-start
  0.0 1.0 %copy.5 = f32[1,256,1,256]{3,1,2,0:T(8,128)S(1)} copy(f32[1,256,1,256]{3,2,1,0:T(1,128)} %param.2) | data formatting | bytes 524288
  1.0 0.0 copy-done
  1.0 73.6 %cycle.1 = f32[256,128]{1,0:T(8,128)S(1)} custom-call(f32[256,256]{1,0:T(8,128)S(1)} %bitcast.3, f32[2,8,16,256]{3,2,1,0:T(8,128)S(1)} %copy-done), custom_call_target="tpu_custom_call" | custom-call | flops 1610612736 | bytes 1048576 | tf_op jit(solution)/shard_map/cycle/pallas_call | solution.py:259
  74.7 0.7 copy.7
Async XLA Ops:
  0.0 1.0 %copy-start = (f32[2,8,16,256]{3,2,1,0:T(8,128)S(1)}, f32[2,8,16,256]{3,2,1,0:T(8,128)}, u32[]{:S(2)}) copy-start(f32[2,8,16,256]{3,2,1,0:T(8,128)} %right_ref.1) | copy-start | bytes 786436

commit v3 on v2

--- a/solution.py
+++ b/solution.py
@@ -61,12 +61,14 @@
     c = lax.broadcasted_iota(jnp.int32, (256, 512), 0)
     t = lax.broadcasted_iota(jnp.int32, (256, 512), 1)
     place = (c // 32) % 4 * 128 + c // 128 * 32 + c % 32
-    pick = [(t == place + shift).astype(F32).astype(BF16) for shift in (0, 64)]
     quarters = jnp.zeros((128, 512), F32)
     for i in range(2):
-        begin = pl.multiple_of(128 * (zh if i == 0 else 1 - zh), 128)
-        high, low = split(left_ref[pl.ds(begin, 128), :])
-        quarters += dot(high, pick[i]) + dot(low, pick[i])
+        pick = (t == place + 64 * i).astype(F32).astype(BF16)
+        for lanes in range(2):
+            begin = 256 * (zh if i == 0 else 1 - zh) + lanes
+            high, low = split(left_ref[pl.ds(begin, 128, stride=2), :])
+            chosen = pick[128 * lanes : 128 * lanes + 128]
+            quarters += dot(high, chosen) + dot(low, chosen)
     for q in range(4):
         packed[q] = quarters[:, 128 * q : 128 * q + 128]
 
@@ -105,7 +107,7 @@
     def spread(half):
         mine = pl.ds(pl.multiple_of(16 * y + 8 * core, 8), 8)
         dst = rows_here.at[half, :, mine, :]
-        for dy in (1, 7, 2, 6, 3, 5, 4, 0):
+        for dy in (4, 3, 5, 2, 6, 1, 7, 0):
             for de in range(2):
                 ty, te = (y + dy) % 8, (core + de) % 2
                 src = pieces.at[half, ty, te]
@@ -124,22 +126,23 @@
             else:
                 pltpu.make_async_copy(src, dst, third_recv.at[half]).start()
 
-    spread(0)
     goes = (x1 != zh).astype(jnp.int32)
     for dx in range(4):
         tx = (x + dx) % 4
         dst = stage.at[goes, x0]
         if dx:
-            start(packed.at[tx], dst, pack_send.at[dx], pack_recv.at[goes], (tx, z, y, core))
+            start(packed.at[tx], dst, pack_send.at[dx], pack_recv.at[goes, x0], (tx, z, y, core))
         else:
-            pltpu.make_async_copy(packed.at[tx], dst, pack_recv.at[goes]).start()
+            pltpu.make_async_copy(packed.at[tx], dst, pack_recv.at[goes, x0]).start()
+    spread(0)
     spread(1)
-    arrive(stage.at[1], pack_recv.at[1])
-    start(stage.at[1], far, far_send, far_recv, (x, (z + 4) % 8, y, core))
-    arrive(rows_here.at[0], spread_recv.at[0])
-    spread_x(0)
-    arrive(rows_here.at[1], spread_recv.at[1])
-    spread_x(1)
+    for f in range(2):
+        arrive(stage.at[1, f], pack_recv.at[1, f])
+        start(stage.at[1, f], far.at[f], far_send.at[f], far_recv.at[f], (x, (z + 4) % 8, y, core))
+
+    for half in range(2):
+        arrive(rows_here.at[half], spread_recv.at[half])
+        spread_x(half)
 
     yr, yl, zr, zlft = (y + 1) % RING, (y + 7) % RING, (z + 1) % RING, (z + 7) % RING
 
@@ -175,10 +178,10 @@
         send_z(z, h, 1 - h, 0)
 
     ring_z_begin(0)
-    arrive(stage.at[0], pack_recv.at[0])
-    arrive(far, far_recv)
     low_lane = lax.broadcasted_iota(jnp.int32, (128, 128), 1) < 64
     for f in range(2):
+        arrive(stage.at[0, f], pack_recv.at[0, f])
+        arrive(far.at[f], far_recv.at[f])
         near_part, far_part = stage[0, f], far[f]
         even = jnp.where(zh == 0, near_part, far_part)
         odd = jnp.where(zh == 0, far_part, near_part)
@@ -211,18 +214,29 @@
                 shared.append((slot_y, h))
                 split_right(slot, h)
                 split_left(slot_y, core, h)
-    for number, (slot_y, h) in enumerate(shared):
+    def take_shared(number):
+        slot_y, h = shared[number]
         arrive(left_all.at[slot_y, 1 - core, h], share_recv.at[number])
         split_left(slot_y, 1 - core, h)
 
-    for f in range(2):
-        total = jnp.zeros((256, 256), F32)
-        for unit in range(8):
-            lh, ll, rh, rl = left_hi[unit, f], left_lo[unit, f], right_hi[unit], right_lo[unit]
-            total += dot(lh, rh) + dot(lh, rl) + dot(ll, rh)
+    def product(unit, f):
+        lh, ll, rh, rl = left_hi[unit, f], left_lo[unit, f], right_hi[unit], right_lo[unit]
+        return dot(lh, rh) + dot(lh, rl) + dot(ll, rh)
+
+    for number in range(14):
+        take_shared(number)
+    for f in range(2):
+        total = product((y + 5) % 8, f)
+        for step in range(6, 12):
+            total += product((y + step) % 8, f)
         for half in range(2):
             partial[f, half] = total[:, 128 * half : 128 * half + 128]
-        for dx in range(1, 4):
+    for f in range(2):
+        take_shared(14 + f)
+        total = product((y + 4) % 8, f)
+        for half in range(2):
+            partial[f, half] += total[:, 128 * half : 128 * half + 128]
+        for dx in (2, 1, 3):
             tx = (x + dx) % 4
             src = partial.at[f, :, pl.ds(pl.multiple_of(64 * tx, 64), 64), :]
             start(src, arrived.at[dx - 1, f], part_send.at[dx - 1, f], part_recv.at[dx - 1, f], (tx, z, y, core))
@@ -233,15 +247,15 @@
         kept = partial[f, :, pl.ds(pl.multiple_of(64 * x, 64), 64), :]
         summed[f] = kept + arrived[0, f] + arrived[1, f] + arrived[2, f]
         for half in range(2):
-            src = summed.at[f, half]
             to = (2 * half + y // 4, zh * 4 + y % 4, 4 * f + zl, x // 2)
             dst = mirror.at[core, pl.ds(pl.multiple_of(64 * x0, 64), 64)]
             home = (to[0] == x) & (to[1] == z) & (to[2] == y) & (to[3] == core)
-            start_or_keep(home, src, dst, mirror_send.at[f, half], mirror_recv, to)
+            start_or_keep(home, summed.at[f, half], dst, mirror_send.at[f, half], mirror_recv, to)
+        for half in range(2):
             to = (2 * zh + f, half * 4 + zl, y, core)
             dst = own.at[pl.ds(pl.multiple_of(64 * x, 64), 64)]
             home = (to[0] == x) & (to[1] == z)
-            start_or_keep(home, src, dst, own_send.at[f, half], own_recv, to)
+            start_or_keep(home, summed.at[f, half], dst, own_send.at[f, half], own_recv, to)
 
     arrive(own, own_recv)
     arrive(mirror, mirror_recv)
@@ -278,8 +292,8 @@
             pltpu.VMEM((2, 2, 64, 128), F32),
             pltpu.VMEM((256, 128), F32),
             pltpu.VMEM((2, 128, 128), F32),
-            dma((4,)), dma((2,)),
-            dma, dma,
+            dma((4,)), dma((2, 2)),
+            dma((2,)), dma((2,)),
             dma((2, 16)), dma((2,)),
             dma((2, 4)), dma((2,)),
             dma((2, 4, 2)), dma((2, 4, 2)),
@@ -294,7 +308,7 @@
         ),
         cost_estimate=pl.CostEstimate(flops=3 * 2**29, bytes_accessed=1 << 20, transcendentals=0),
         name="cycle",
-    )(integrals.reshape(256, 256), amplitudes)
+    )(integrals.reshape(512, 128), amplitudes)
 
 
 def solution(mesh):

time: 75.7 us -> 73.1 us (0.966)
  Pallas kernels: 73.6 us -> 69.6 us
  local copies, waits for them, and re-layouts: 1.68 us -> 2.56 us
    pallas_call x1, Pallas kernels: 73.6 us -> 69.6 us  [body(): pl.pallas_call(kernel, out_shape=jax.ShapeDtypeStruct((256, 128), F32), i...]
    unnamed x4 -> x5, local copies, waits for them, and re-layouts: 1.68 us -> 2.56 us
where the time goes in v3:
time: 73.1 us; the launch traced here: 72.2 us
  Pallas kernels  69.6 us (95%)
  local copies, waits for them, and re-layouts  2.56 us (4%)
    pallas_call x1, Pallas kernels, body(): pl.pallas_call(kernel, out_shape=jax.ShapeDtypeStruct((256, 128), F32), i...  69.6 us
    unnamed x5, local copies, waits for them, and re-layouts  2.56 us

profile of v3, /device:TPU:57, one launch (start us, length us, event | category | flops | bytes accessed | tf_op | source)
XLA Modules:
  0.0 72.2 jit_solution(8728042747858675129)
XLA Ops:
  0.0 0.0 copy-start
  0.0 0.9 %copy-done = f32[1,256,1,256]{3,2,1,0:T(1,128)S(1)} copy-done((f32[1,256,1,256]{3,2,1,0:T(1,128)S(1)}, f32[1,256,1,256]{3,2,1,0:T(1,128)}, u32[]{:S(2)}) %copy-start) | copy-done | bytes 262168
  1.0 0.0 copy-start.1
  1.0 0.9 %copy-done.1 = f32[2,8,16,256]{3,2,1,0:T(8,128)S(1)} copy-done((f32[2,8,16,256]{3,2,1,0:T(8,128)S(1)}, f32[2,8,16,256]{3,2,1,0:T(8,128)}, u32[]{:S(2)}) %copy-start.1) | copy-done | bytes 262168
  1.9 69.6 %cycle.1 = f32[256,128]{1,0:T(8,128)S(1)} custom-call(f32[512,128]{1,0:T(8,128)S(1)} %bitcast.1, f32[2,8,16,256]{3,2,1,0:T(8,128)S(1)} %copy-done.1), custom_call_target="tpu_custom_call" | custom-call | flops 1610612736 | bytes 1048576 | tf_op jit(solution)/shard_map/cycle/pallas_call | solution.py:273
  71.5 0.7 copy.4
Async XLA Ops:
  0.0 0.9 %copy-start = (f32[1,256,1,256]{3,2,1,0:T(1,128)S(1)}, f32[1,256,1,256]{3,2,1,0:T(1,128)}, u32[]{:S(2)}) copy-start(f32[1,256,1,256]{3,2,1,0:T(1,128)} %param.2) | copy-start | bytes 786436
  1.0 0.9 %copy-start.1 = (f32[2,8,16,256]{3,2,1,0:T(8,128)S(1)}, f32[2,8,16,256]{3,2,1,0:T(8,128)}, u32[]{:S(2)}) copy-start(f32[2,8,16,256]{3,2,1,0:T(8,128)} %right_ref.1) | copy-start | bytes 786436

commit v4 on v3

--- a/solution.py
+++ b/solution.py
@@ -58,19 +58,19 @@
                 for j in range(8):
                     pieces[half, j, e, k] = block[j]
 
-    c = lax.broadcasted_iota(jnp.int32, (256, 512), 0)
-    t = lax.broadcasted_iota(jnp.int32, (256, 512), 1)
-    place = (c // 32) % 4 * 128 + c // 128 * 32 + c % 32
-    quarters = jnp.zeros((128, 512), F32)
+    lane = lax.broadcasted_iota(jnp.int32, (128, 128), 1)
+    strips = []
     for i in range(2):
-        pick = (t == place + 64 * i).astype(F32).astype(BF16)
         for lanes in range(2):
             begin = 256 * (zh if i == 0 else 1 - zh) + lanes
-            high, low = split(left_ref[pl.ds(begin, 128, stride=2), :])
-            chosen = pick[128 * lanes : 128 * lanes + 128]
-            quarters += dot(high, chosen) + dot(low, chosen)
+            strips.append(left_ref[pl.ds(begin, 128, stride=2), :])
     for q in range(4):
-        packed[q] = quarters[:, 128 * q : 128 * q + 128]
+        turned = [pltpu.roll(strip, (32 * i - 32 * q) % 128, 1) if i != q else strip for i, strip in enumerate(strips)]
+        packed[q] = jnp.where(
+            lane < 64,
+            jnp.where(lane < 32, turned[0], turned[1]),
+            jnp.where(lane < 96, turned[2], turned[3]),
+        )
 
     pl.semaphore_wait(barrier, 21)
 
@@ -178,7 +178,7 @@
         send_z(z, h, 1 - h, 0)
 
     ring_z_begin(0)
-    low_lane = lax.broadcasted_iota(jnp.int32, (128, 128), 1) < 64
+    low_lane = lane < 64
     for f in range(2):
         arrive(stage.at[0, f], pack_recv.at[0, f])
         arrive(far.at[f], far_recv.at[f])
@@ -195,35 +195,40 @@
     for h in range(2):
         split_right(z, h)
         split_left(y, core, h)
+    def take_shared(number):
+        slot_y, h = shared[number]
+        arrive(left_all.at[slot_y, 1 - core, h], share_recv.at[number])
+        split_left(slot_y, 1 - core, h)
+
     for step in range(4):
-        for i in range(2):
+        for i in range(2 if step < 3 else 1):
+            last = step == 3 or (step == 2 and i == 1)
+            come = []
             for way in range(2):
                 h = i if way == 0 else 1 - i
-                if step == 3 and i == 1:
-                    continue
-                last = step == 3 or (step == 2 and i == 1)
-                slot = (z - 1 - step + 8) % 8 if way == 0 else (z + 1 + step) % 8
-                arrive(right_all.at[slot, h], zrecv.at[way, step, h])
-                if not last:
-                    send_z(slot, h, way, step + 1)
                 slot_y = (y - 1 - step + 8) % 8 if way == 0 else (y + 1 + step) % 8
                 arrive(left_all.at[slot_y, core, h], yrecv.at[way, step, h])
                 if not last:
                     send_y(slot_y, h, way, step + 1)
                 share(slot_y, h, len(shared))
                 shared.append((slot_y, h))
+                slot = (z - 1 - step + 8) % 8 if way == 0 else (z + 1 + step) % 8
+                arrive(right_all.at[slot, h], zrecv.at[way, step, h])
+                if not last:
+                    send_z(slot, h, way, step + 1)
+                come.append((slot_y, slot, h))
+            for slot_y, slot, h in come:
+                split_left(slot_y, core, h)
                 split_right(slot, h)
-                split_left(slot_y, core, h)
-    def take_shared(number):
-        slot_y, h = shared[number]
-        arrive(left_all.at[slot_y, 1 - core, h], share_recv.at[number])
-        split_left(slot_y, 1 - core, h)
+            if len(shared) > 4:
+                take_shared(len(shared) - 6)
+                take_shared(len(shared) - 5)
 
     def product(unit, f):
         lh, ll, rh, rl = left_hi[unit, f], left_lo[unit, f], right_hi[unit], right_lo[unit]
         return dot(lh, rh) + dot(lh, rl) + dot(ll, rh)
 
-    for number in range(14):
+    for number in range(12, 14):
         take_shared(number)
     for f in range(2):
         total = product((y + 5) % 8, f)

time: 73.1 us -> 72.6 us (level)
  no operation moved by 1% of the time
where the time goes in v4:
time: 72.6 us; the launch traced here: 71.7 us
  Pallas kernels  69.2 us (95%)
  local copies, waits for them, and re-layouts  2.56 us (4%)
    pallas_call x1, Pallas kernels, body(): pl.pallas_call(kernel, out_shape=jax.ShapeDtypeStruct((256, 128), F32), i...  69.2 us
    unnamed x5, local copies, waits for them, and re-layouts  2.56 us

profile of v4, /device:TPU:57, one launch (start us, length us, event | category | flops | bytes accessed | tf_op | source)
XLA Modules:
  0.0 71.7 jit_solution(15279003443603089531)
XLA Ops:
  0.0 0.0 copy-start
  0.0 0.9 %copy-done = f32[1,256,1,256]{3,2,1,0:T(1,128)S(1)} copy-done((f32[1,256,1,256]{3,2,1,0:T(1,128)S(1)}, f32[1,256,1,256]{3,2,1,0:T(1,128)}, u32[]{:S(2)}) %copy-start) | copy-done | bytes 262168
  1.0 0.0 copy-start.1
  1.0 0.9 %copy-done.1 = f32[2,8,16,256]{3,2,1,0:T(8,128)S(1)} copy-done((f32[2,8,16,256]{3,2,1,0:T(8,128)S(1)}, f32[2,8,16,256]{3,2,1,0:T(8,128)}, u32[]{:S(2)}) %copy-start.1) | copy-done | bytes 262168
  1.9 69.2 %cycle.1 = f32[256,128]{1,0:T(8,128)S(1)} custom-call(f32[512,128]{1,0:T(8,128)S(1)} %bitcast.1, f32[2,8,16,256]{3,2,1,0:T(8,128)S(1)} %copy-done.1), custom_call_target="tpu_custom_call" | custom-call | flops 1610612736 | bytes 1048576 | tf_op jit(solution)/shard_map/cycle/pallas_call | solution.py:278
  71.1 0.7 copy.4
Async XLA Ops:
  0.0 0.9 %copy-start = (f32[1,256,1,256]{3,2,1,0:T(1,128)S(1)}, f32[1,256,1,256]{3,2,1,0:T(1,128)}, u32[]{:S(2)}) copy-start(f32[1,256,1,256]{3,2,1,0:T(1,128)} %param.2) | copy-start | bytes 786436
  1.0 0.9 %copy-start.1 = (f32[2,8,16,256]{3,2,1,0:T(8,128)S(1)}, f32[2,8,16,256]{3,2,1,0:T(8,128)}, u32[]{:S(2)}) copy-start(f32[2,8,16,256]{3,2,1,0:T(8,128)} %right_ref.1) | copy-start | bytes 786436

commit v5 on v4

--- a/solution.py
+++ b/solution.py
@@ -62,8 +62,8 @@
     strips = []
     for i in range(2):
         for lanes in range(2):
-            begin = 256 * (zh if i == 0 else 1 - zh) + lanes
-            strips.append(left_ref[pl.ds(begin, 128, stride=2), :])
+            begin = pl.multiple_of(128 * (zh if i == 0 else 1 - zh), 128)
+            strips.append(left_ref[pl.ds(begin, 128), 128 * lanes : 128 * lanes + 128])
     for q in range(4):
         turned = [pltpu.roll(strip, (32 * i - 32 * q) % 128, 1) if i != q else strip for i, strip in enumerate(strips)]
         packed[q] = jnp.where(
@@ -313,7 +313,7 @@
         ),
         cost_estimate=pl.CostEstimate(flops=3 * 2**29, bytes_accessed=1 << 20, transcendentals=0),
         name="cycle",
-    )(integrals.reshape(512, 128), amplitudes)
+    )(integrals.reshape(256, 256), amplitudes)
 
 
 def solution(mesh):

time: 72.6 us -> 71.7 us (0.988)
  local copies, waits for them, and re-layouts: 2.56 us -> 1.68 us
    unnamed x5 -> x4, local copies, waits for them, and re-layouts: 2.56 us -> 1.68 us
where the time goes in v5:
time: 71.7 us; the launch traced here: 70.8 us
  Pallas kernels  69.2 us (97%)
  local copies, waits for them, and re-layouts  1.68 us (2%)
    pallas_call x1, Pallas kernels, body(): pl.pallas_call(kernel, out_shape=jax.ShapeDtypeStruct((256, 128), F32), i...  69.2 us
    unnamed x4, local copies, waits for them, and re-layouts  1.68 us

profile of v5, /device:TPU:57, one launch (start us, length us, event | category | flops | bytes accessed | tf_op | source)
XLA Modules:
  0.0 70.8 jit_solution(8354701536298874175)
XLA Ops:
  0.0 0.0 copy-start
  0.0 1.0 %copy.5 = f32[1,256,1,256]{3,1,2,0:T(8,128)S(1)} copy(f32[1,256,1,256]{3,2,1,0:T(1,128)} %param.2) | data formatting | bytes 524288
  1.0 0.0 copy-done
  1.0 69.2 %cycle.1 = f32[256,128]{1,0:T(8,128)S(1)} custom-call(f32[256,256]{1,0:T(8,128)S(1)} %bitcast.3, f32[2,8,16,256]{3,2,1,0:T(8,128)S(1)} %copy-done), custom_call_target="tpu_custom_call" | custom-call | flops 1610612736 | bytes 1048576 | tf_op jit(solution)/shard_map/cycle/pallas_call | solution.py:278
  70.2 0.7 copy.7
Async XLA Ops:
  0.0 1.0 %copy-start = (f32[2,8,16,256]{3,2,1,0:T(8,128)S(1)}, f32[2,8,16,256]{3,2,1,0:T(8,128)}, u32[]{:S(2)}) copy-start(f32[2,8,16,256]{3,2,1,0:T(8,128)} %right_ref.1) | copy-start | bytes 786436
